TPU v7x, 256 devices: a whole 4x4x8 slice. The times are simulated.
256 devices in a mesh: section: 8 (over z_lo, core), tensor: 32 (over z_hi, y, x).
Axes of the slice: x: 4, y: 4, z: 8 (z_hi: 2, z_lo: 4; z = z_hi * 4 + z_lo), core: 2. Of those that a mesh axis runs over, the one named last changes fastest.
Arguments:
- held: bfloat16 [8, 4, 256, 2048], P('section', None, 'tensor'), may hold values from -6 to 6
- head: bfloat16 [4, 256, 2048], P(None, 'tensor'), may hold values from -6 to 6
- gains: float32 [8, 2, 2048], P('section'), may hold values from 0.1 to 1.9
- w_in: bfloat16 [8, 2, 2048, 8192], P('section', None, None, 'tensor'), may hold values from -0.125 to 0.125
- w_out: bfloat16 [8, 2, 8192, 2048], P('section', None, 'tensor'), may hold values from -0.0625 to 0.0625
- masks: int32 [8, 2, 2, 256, 8192], P('section', None, None, None, 'tensor'), may hold values 0 or 1
Outputs:
- rebuilt: bfloat16 [8, 2, 4, 256, 2048], P('section', None, None, 'tensor')
- grad_w_in: bfloat16 [8, 2, 2048, 8192], P('section', None, None, 'tensor')
- grad_w_out: bfloat16 [8, 2, 8192, 2048], P('section', None, 'tensor')
- grad_gains: float32 [8, 2, 2048], P('section')
Inputs may be any that keep to these rules, and one draw needn't show every extreme that they name: `masks`: 1 keeps a hidden unit, 0 drops it.
All inputs are finite; a program needn't handle non-finite values. No bound on the sum of `masks` on one device may be relied on, other than what follows from the above.
Results may differ from a plain program's by a relative error of at most 0.04.
Values may be sent and summed in bfloat16 or wider, within the bound.
A program may use at most 128 MiB of HBM per device.

v0:
```python
import math

import jax
import jax.numpy as jnp
from jax import lax
from jax.sharding import PartitionSpec as P

KEEP = 0.9
EPS = 1e-05
CUBIC = 0.044715
ROOT = math.sqrt(2.0 / math.pi)


def from_behind(x, axis, by):
    size = lax.axis_size(axis)
    pairs = [(i, i + by) for i in range(size) if 0 <= i + by < size]
    return lax.ppermute(x, axis, pairs)


def gelu_value(hidden):
    inner = ROOT * (hidden + CUBIC * hidden * hidden * hidden)
    return 0.5 * hidden * (1.0 + jnp.tanh(inner))


def gelu_slope(hidden):
    inner = ROOT * (hidden + CUBIC * hidden * hidden * hidden)
    tangent = jnp.tanh(inner)
    return 0.5 * (1.0 + tangent) + 0.5 * hidden * (1.0 - tangent * tangent) * ROOT * (
        1.0 + 3.0 * CUBIC * hidden * hidden
    )


def branch_forward(inputs, gain, w_first, w_second, mask):
    wide = inputs.astype(jnp.float32)
    scale = lax.rsqrt(jnp.mean(wide * wide, axis=-1, keepdims=True) + EPS)
    unit = wide * scale
    normed = (unit * gain).astype(jnp.bfloat16)
    hidden = jnp.dot(normed, w_first, preferred_element_type=jnp.float32)
    keep_mask = mask.astype(jnp.float32) / KEEP
    active = (gelu_value(hidden) * keep_mask).astype(jnp.bfloat16)
    partial_sum = jnp.dot(active, w_second, preferred_element_type=jnp.float32)
    branch = lax.psum(partial_sum.astype(jnp.bfloat16), "tensor").astype(jnp.float32)
    return (branch, (scale, unit, normed, hidden, keep_mask, active))


def branch_backward(grad, gain, w_first, w_second, saved):
    scale, unit, gathered, hidden, keep_mask, active = saved
    back_active = lax.dot_general(
        grad, w_second, (((1,), (1,)), ((), ())), preferred_element_type=jnp.float32
    )
    back_hidden = (back_active * keep_mask * gelu_slope(hidden)).astype(jnp.bfloat16)
    term_out = lax.dot_general(
        active, grad, (((0,), (0,)), ((), ())), preferred_element_type=jnp.float32
    )
    term_in = lax.dot_general(
        gathered, back_hidden, (((0,), (0,)), ((), ())), preferred_element_type=jnp.float32
    )
    partial_sum = lax.dot_general(
        back_hidden, w_first, (((1,), (1,)), ((), ())), preferred_element_type=jnp.float32
    )
    back_normed = lax.psum(partial_sum.astype(jnp.bfloat16), "tensor").astype(jnp.float32)
    term_gain = jnp.sum(back_normed * unit, axis=0)
    back_unit = back_normed * gain
    back_input = scale * (back_unit - unit * jnp.mean(back_unit * unit, axis=-1, keepdims=True))
    return (back_input, term_in, term_out, term_gain)


def section_backward(inputs, gain, w_first, w_second, mask):
    out_one, out_two, grad_one, grad_two = (inputs[0], inputs[1], inputs[2], inputs[3])
    branch_two, saved_two = branch_forward(out_one, gain[1], w_first[1], w_second[1], mask[1])
    in_two = (out_two.astype(jnp.float32) - branch_two).astype(jnp.bfloat16)
    branch_one, saved_one = branch_forward(in_two, gain[0], w_first[0], w_second[0], mask[0])
    in_one = (out_one.astype(jnp.float32) - branch_one).astype(jnp.bfloat16)
    back_two, in_b, out_b, gain_b = branch_backward(
        grad_two, gain[1], w_first[1], w_second[1], saved_two
    )
    grad_in_one = (grad_one.astype(jnp.float32) + back_two).astype(jnp.bfloat16)
    back_one, in_a, out_a, gain_a = branch_backward(
        grad_in_one, gain[0], w_first[0], w_second[0], saved_one
    )
    grad_in_two = (grad_two.astype(jnp.float32) + back_one).astype(jnp.bfloat16)
    rebuilt = jnp.stack([in_one, in_two, grad_in_one, grad_in_two])
    return (
        rebuilt,
        jnp.stack([in_a, in_b]),
        jnp.stack([out_a, out_b]),
        jnp.stack([gain_a, gain_b]),
    )


def run_tick(local_rows, gain, w_first, w_second, mask):
    whole = lax.all_gather(local_rows, "tensor", axis=1, tiled=True)
    rebuilt, term_in, term_out, term_gain = section_backward(whole, gain, w_first, w_second, mask)
    count = local_rows.shape[1]
    rebuilt = lax.dynamic_slice_in_dim(rebuilt, lax.axis_index("tensor") * count, count, 1)
    return (rebuilt, term_in, term_out, term_gain)


def per_device(held, head, gains, w_in, w_out, masks):
    gain = gains[0]
    w_first = w_in[0]
    w_second = w_out[0]
    is_last = lax.axis_index("section") == lax.axis_size("section") - 1
    first, in_a, out_a, gain_a = run_tick(held[0], gain, w_first, w_second, masks[0, 0])
    arrived = from_behind(first, "section", -1)
    source = jnp.where(is_last, head, arrived)
    second, in_b, out_b, gain_b = run_tick(source, gain, w_first, w_second, masks[0, 1])
    gain_total = gain_a + gain_b
    rebuilt = jnp.stack([first, second])[None]
    grad_first = (in_a + in_b).astype(jnp.bfloat16)[None]
    grad_second = (out_a + out_b).astype(jnp.bfloat16)[None]
    return (rebuilt, grad_first, grad_second, gain_total[None])


def solution(mesh):
    return jax.shard_map(
        per_device,
        mesh=mesh,
        in_specs=(
            P("section", None, "tensor", None),
            P(None, "tensor", None),
            P("section", None, None),
            P("section", None, None, "tensor"),
            P("section", None, "tensor", None),
            P("section", None, None, None, "tensor"),
        ),
        out_specs=(
            P("section", None, None, "tensor", None),
            P("section", None, None, "tensor"),
            P("section", None, "tensor", None),
            P("section", None, None),
        ),
        check_vma=False,
    )
```

profile of v0, /device:TPU:64, one launch (start us, length us, event | category | flops | bytes accessed | tf_op | source)
XLA Modules:
  0.0 2029.2 jit_solution(11490438748407930279)
XLA Ops:
  8.8 115.5 %all-gather.6.cloned.1.call-done = bf16[1,4,256,2048]{3,2,1,0:T(8,128)(2,1)} async-done(((bf16[1,4,8,2048]{3,2,1,0:T(8,128)(2,1)}), bf16[1,4,256,2048]{3,2,1,0:T(8,128)(2,1)}) %all-gather.6.cloned.1.call-update) | async-done | bytes 4194320 | tf_op jit(solution)/shard_map/all_gather | solution.py:92
  124.3 1.5 fusion.56
  125.8 2.3 fusion.156
  128.1 2.0 fusion.67
  130.2 1.4 convolution_convert_fusion.5
  133.1 428.4 %all-reduce.15.cloned.1.call-done = (bf16[256,2048]{1,0:T(8,128)(2,1)}, bf16[256,2048]{1,0:T(8,128)(2,1)}) async-done(((bf16[256,2048]{1,0:T(8,128)(2,1)}, bf16[256,2048]{1,0:T(8,128)(2,1)}), (bf16[256,2048]{1,0:T(8,128)(2,1)}, bf16[256,2048]{1,0:T(8,128)(2,1)})) %all-reduce.15.cloned.1.call-update) | async-done | bytes 2097168 | tf_op jit(solution)/shard_map/psum | solution.py:42
  561.5 3.1 fusion.55
  564.6 3.4 fusion.40
  570.3 1.4 convolution_convert_fusion.4
  573.2 434.2 %all-reduce.13.cloned.1.call-done = (bf16[256,2048]{1,0:T(8,128)(2,1)}, bf16[256,2048]{1,0:T(8,128)(2,1)}) async-done(((bf16[256,2048]{1,0:T(8,128)(2,1)}, bf16[256,2048]{1,0:T(8,128)(2,1)}), (bf16[256,2048]{1,0:T(8,128)(2,1)}, bf16[256,2048]{1,0:T(8,128)(2,1)})) %all-reduce.13.cloned.1.call-update) | async-done | bytes 2097168 | tf_op jit(solution)/shard_map/psum | solution.py:61
  1007.4 2.8 fusion.41
  1010.2 2.8 fusion.74
  1014.4 1.9 collective-permute-start
  1016.3 2.5 collective-permute-done
  1019.5 112.6 %all-gather.4.cloned.1.call-done = bf16[4,256,2048]{2,1,0:T(8,128)(2,1)} async-done(((bf16[4,8,2048]{2,1,0:T(8,128)(2,1)}), bf16[4,256,2048]{2,1,0:T(8,128)(2,1)}) %all-gather.4.cloned.1.call-update) | async-done | bytes 4194320 | tf_op jit(solution)/shard_map/all_gather | solution.py:92
  1132.1 1.5 fusion.49
  1133.7 2.3 fusion.154
  1136.0 2.0 fusion.69
  1138.0 1.5 convolution_convert_fusion.1
  1141.2 3.1 convolution_bitcast_fusion.6
  1144.3 425.2 %all-reduce.11.cloned.1.call-done = (bf16[256,2048]{1,0:T(8,128)(2,1)}, bf16[256,2048]{1,0:T(8,128)(2,1)}) async-done(((bf16[256,2048]{1,0:T(8,128)(2,1)}, bf16[256,2048]{1,0:T(8,128)(2,1)}), (bf16[256,2048]{1,0:T(8,128)(2,1)}, bf16[256,2048]{1,0:T(8,128)(2,1)})) %all-reduce.11.cloned.1.call-update) | async-done | bytes 2097168 | tf_op jit(solution)/shard_map/psum | solution.py:42
  1569.5 3.1 fusion.48
  1572.7 3.4 fusion.44
  1578.8 1.5 convolution_convert_fusion
  1580.2 1.4 convolution_convert_fusion.2
  1581.7 1.7 convolution_bitcast_fusion.2
  1585.6 2.2 copy-done
  1592.4 1.8 fusion
  1594.2 1.9 fusion.1
  1596.2 419.7 %all-reduce.9.cloned.1.call-done = (bf16[256,2048]{1,0:T(8,128)(2,1)}, bf16[256,2048]{1,0:T(8,128)(2,1)}) async-done(((bf16[256,2048]{1,0:T(8,128)(2,1)}, bf16[256,2048]{1,0:T(8,128)(2,1)}), (bf16[256,2048]{1,0:T(8,128)(2,1)}, bf16[256,2048]{1,0:T(8,128)(2,1)})) %all-reduce.9.cloned.1.call-update) | async-done | bytes 2097168 | tf_op jit(solution)/shard_map/psum | solution.py:61
  2015.9 2.2 fusion.45
  2018.2 2.8 fusion.79
  (127 shorter events, 21.4 us)
Async XLA Ops:
  7.2 117.1 %all-gather.6.cloned.1.call-start = ((), (), s32[]{:S(2)}) async-start(), calls=%async_computation.1 | async-start | bytes 4325376 | tf_op jit(solution)/shard_map/all_gather | solution.py:92
  7.9 553.6 %all-reduce.15.cloned.1.call-start = ((), (), s32[]{:S(2)}) async-start(), calls=%async_computation.5 | async-start | bytes 4194304 | tf_op jit(solution)/shard_map/psum | solution.py:42
  125.8 2.3 copy-start.11
  128.1 2.0 copy-start.7
  133.0 874.4 %all-reduce.13.cloned.1.call-start = ((), (), s32[]{:S(2)}) async-start(), calls=%async_computation.4 | async-start | bytes 4194304 | tf_op jit(solution)/shard_map/psum | solution.py:61
  561.5 3.1 copy-start.18
  561.5 3.1 copy-start.23
  564.6 3.4 copy-start.8
  564.6 3.5 copy-start.42
  568.0 442.2 %copy-start.36 = (f32[256]{0:T(256)}, f32[256]{0:T(256)S(1)}, u32[]{:S(2)}) copy-start(f32[256]{0:T(256)S(1)} %add_rsqrt_fusion.2) | copy-start | bytes 3076
  573.2 559.0 %all-gather.4.cloned.1.call-start = ((), (), s32[]{:S(2)}) async-start(), calls=%async_computation | async-start | bytes 4325376 | tf_op jit(solution)/shard_map/all_gather | solution.py:92
  1007.4 2.8 copy-start.16
  1007.4 2.8 copy-start.21
  1013.0 5.8 copy-start.32
  1014.4 4.4 collective-permute-start
  1019.5 550.0 %all-reduce.11.cloned.1.call-start = ((), (), s32[]{:S(2)}) async-start(), calls=%async_computation.3 | async-start | bytes 4194304 | tf_op jit(solution)/shard_map/psum | solution.py:42
  1133.6 435.9 %copy-start.40 = (f32[256]{0:T(256)}, f32[256]{0:T(256)S(1)}, u32[]{:S(2)}) copy-start(f32[256]{0:T(256)S(1)} %add_rsqrt_fusion.1) | copy-start | bytes 3076
  1133.7 2.3 copy-start.13
  1135.9 3.6 copy-start.24
  1136.0 2.1 copy-start.9
  1138.0 2.9 copy-start.30
  1141.0 875.0 %all-reduce.9.cloned.1.call-start = ((), (), s32[]{:S(2)}) async-start(), calls=%async_computation.2 | async-start | bytes 4194304 | tf_op jit(solution)/shard_map/psum | solution.py:61
  1569.5 3.1 copy-start.17
  1569.5 3.1 copy-start.22
  1572.7 3.5 copy-start.10
  1572.7 3.5 copy-start.43
  1576.1 2.0 copy-start.14
  1577.0 3.3 copy-start.26
  1585.6 2.2 copy-start
  1585.6 2.2 copy-start.25
  2015.9 2.2 copy-start.15
  2015.9 2.2 copy-start.20
  (19 other events, 20.7 us)
Sparse Core Ops, SparseCore 0:
  11.4 112.7 all-gather.5
  133.2 428.2 all-reduce.14
  573.3 434.0 all-reduce.12
  1019.6 112.4 all-gather.3
  1141.1 428.4 all-reduce.10
  1581.8 434.0 all-reduce.8
where the time goes:
time: 2030 us
  waiting for transfers between devices  1940 us (96%)
  other arithmetic  32.5 us (2%)
  matrix products  30.4 us (1%)
    psum x2, waiting for transfers between devices, branch_backward(): lax.psum(partial_sum.astype(jnp.bfloat16), 'tensor').astype(jnp.float32)  854 us
    psum x2, waiting for transfers between devices, branch_forward(): lax.psum(partial_sum.astype(jnp.bfloat16), 'tensor').astype(jnp.float32)  854 us
    all_gather x2, waiting for transfers between devices, run_tick(): whole = lax.all_gather(local_rows, 'tensor', axis=1, tiled=True)  228 us
  transfers between devices with their start and end apart: 7, of which 7 were waited for; matrix products, arithmetic and copies ran while one was open for 1% of the time, Pallas kernels for 0%

commit v1 on v0

v1 whole, which is shorter than its diff:
```python
import math

import jax
import jax.numpy as jnp
from jax import lax
from jax.experimental import pallas as pl
from jax.experimental.pallas import tpu as pltpu
from jax.sharding import PartitionSpec as P

KEEP = 0.9
EPS = 1e-05
CUBIC = 0.044715
ROOT = math.sqrt(2.0 / math.pi)
MESH = pl.DeviceIdType.MESH
F32 = jnp.float32
BF16 = jnp.bfloat16
FWD, BWD = 0, 1
HALF = 1024
OFFSETS = (2, 1, 3)


def dot_nn(a, b):
    return lax.dot_general(a, b, (((1,), (0,)), ((), ())), preferred_element_type=F32)


def dot_nt(a, b):
    return lax.dot_general(a, b, (((1,), (1,)), ((), ())), preferred_element_type=F32)


def dot_tn(a, b):
    return lax.dot_general(a, b, (((0,), (0,)), ((), ())), preferred_element_type=F32)


def kernel(
    held, head, gains, w_in_hbm, w_out_hbm, masks_hbm,
    rebuilt, grad_in_hbm, grad_out_hbm, grad_gains,
    w_in, w_out, masks, gath, part, r1, s1, r2, zs, zr, rows, act_t, back_h, slope_k,
    gw_in, gw_out, hs, hr, gsum, grx, gry,
    ag1_s, ag1_r, agx_s, agx_r, ag2_s, ag2_r, rs1_s, rs1_r, rs2_s, rs2_r, z_s, z_r,
    tick_s, tick_r, hs_s, hs_r, gx_s, gx_r, load_s, out_s,
):
    sec = lax.axis_index("section")
    me = lax.axis_index("tensor")
    last = lax.axis_size("section") - 1
    x = lax.rem(me, 4)
    y = lax.rem(me // 4, 4)
    z = me // 16

    def x_peer(d):
        return {"tensor": z * 16 + y * 4 + lax.rem(x + d, 4)}

    def y_peer(d):
        return {"tensor": z * 16 + lax.rem(y + d, 4) * 4 + x}

    z_peer = {"tensor": lax.rem(me + 16, 32)}

    def send(src, dst, s_sem, r_sem, device):
        pltpu.make_async_remote_copy(
            src_ref=src, dst_ref=dst, send_sem=s_sem, recv_sem=r_sem,
            device_id=device, device_id_type=MESH,
        ).start()

    def wait(ref, sem):
        pltpu.make_async_copy(ref, ref, sem).wait()

    loads = [
        pltpu.make_async_copy(w_in_hbm, w_in, load_s.at[0]),
        pltpu.make_async_copy(w_out_hbm, w_out, load_s.at[1]),
    ]
    for dy in range(4):
        for dx in range(4):
            block = lax.rem(y + dy, 4) * 4 + lax.rem(x + dx, 4)
            loads.append(
                pltpu.make_async_copy(
                    masks_hbm.at[:, :, :, block], masks.at[:, :, dy * 4 + dx], load_s.at[2 + dy * 4 + dx]
                )
            )
    for copy in loads:
        copy.start()

    barrier = pltpu.get_barrier_semaphore()
    for d in (1, 2, 3):
        pl.semaphore_signal(barrier, inc=1, device_id=x_peer(d), device_id_type=MESH)
        pl.semaphore_signal(barrier, inc=1, device_id=y_peer(d), device_id_type=MESH)
    pl.semaphore_signal(barrier, inc=1, device_id=z_peer, device_id_type=MESH)

    above = {"section": lax.rem(sec + 1, last + 1)}
    pl.semaphore_signal(barrier, inc=1, device_id=above, device_id_type=MESH)

    def pack(source, slot):
        for j in range(4):
            v = source[j].astype(F32)
            hs[slot, j] = jnp.concatenate([v[:, :HALF], v[:, HALF:]], axis=0).astype(BF16)

    pack(held, 0)

    pl.semaphore_wait(barrier, 8)

    places = ((0, FWD, 1), (3, BWD, 1), (1, FWD, 0), (2, BWD, 0))
    for j, _, _ in places:
        send(hs.at[0, j], hr.at[0, j], hs_s.at[j], hs_r.at[j], z_peer)

    @pl.when(sec == last)
    def _():
        pack(head, 1)
        for j, _, _ in places:
            send(hs.at[1, j], hr.at[1, j], hs_s.at[4 + j], hs_r.at[4 + j], z_peer)

    def unpack(slot, j, tick, chain, place):
        wait(hr.at[slot, j], hs_r.at[4 * slot + j])
        mine = hs[slot, j].astype(F32)
        theirs = hr[slot, j].astype(F32)
        for h in range(2):
            a = mine[8 * h : 8 * h + 8]
            b = theirs[8 * h : 8 * h + 8]
            both = jnp.concatenate([jnp.where(z == 0, a, b), jnp.where(z == 0, b, a)], axis=0)
            rows[tick, chain, place, h] = both.astype(BF16)

    def gain_row(layer):
        pair = gains[0]
        return jnp.where(layer == 1, pair[1:2], pair[0:1])

    def norm_of(tick, place):
        v0 = rows[tick, FWD, place, 0].astype(F32)
        v1 = rows[tick, FWD, place, 1].astype(F32)
        total = jnp.sum(v0 * v0, axis=-1, keepdims=True) + jnp.sum(v1 * v1, axis=-1, keepdims=True)
        scale = lax.rsqrt(total * (1.0 / (2 * HALF)) + EPS)
        return scale, (v0 * scale, v1 * scale)

    def gather_start(chain, s):
        for d in OFFSETS:
            send(gath.at[s, chain, 0, 0, 0], gath.at[s, chain, 0, 0, 4 - d], ag1_s.at[chain, 0], ag1_r.at[chain, 0], x_peer(d))
            send(gath.at[s, chain, 1, 0, 0], gath.at[s, chain, 1, 4 - d, 0], ag1_s.at[chain, 1], ag1_r.at[chain, 1], y_peer(d))
        for d in OFFSETS:
            send(gath.at[s, chain, 0, 0, 0], gath.at[s, chain, 0, 4 - d, 0], agx_s.at[chain, 0], agx_r.at[chain, 0], y_peer(d))
            send(gath.at[s, chain, 1, 0, 0], gath.at[s, chain, 1, 0, 4 - d], agx_s.at[chain, 1], agx_r.at[chain, 1], x_peer(d))

    def gather_mid(chain, s):
        wait(gath.at[s, chain, 0, 0, pl.ds(1, 3)], ag1_r.at[chain, 0])
        for d in OFFSETS:
            send(
                gath.at[s, chain, 0, 0, pl.ds(1, 3)], gath.at[s, chain, 0, 4 - d, pl.ds(1, 3)],
                ag2_s.at[chain, 0], ag2_r.at[chain, 0], y_peer(d),
            )
        wait(gath.at[s, chain, 1, pl.ds(1, 3), 0], ag1_r.at[chain, 1])
        for d in OFFSETS:
            send(
                gath.at[s, chain, 1, pl.ds(1, 3), 0], gath.at[s, chain, 1, pl.ds(1, 3), 4 - d],
                ag2_s.at[chain, 1], ag2_r.at[chain, 1], x_peer(d),
            )

    def gather_wait(chain, s, h):
        wait(gath.at[s, chain, h, 0, pl.ds(1, 3)], agx_r.at[chain, h])
        wait(gath.at[s, chain, h, pl.ds(1, 3), pl.ds(1, 3)], ag2_r.at[chain, h])

    def gather_sent(chain, s):
        for h in range(2):
            wait(gath.at[s, chain, h, 0, pl.ds(1, 3)], ag1_s.at[chain, h])
            wait(gath.at[s, chain, h, 0, pl.ds(1, 3)], agx_s.at[chain, h])
            wait(gath.at[s, chain, h, pl.ds(1, 3), pl.ds(1, 3)], ag2_s.at[chain, h])

    def gathered(chain, s, h):
        return gath[s, chain, h].reshape(256, HALF)

    def put_part(chain, h, value):
        part[chain, h] = value.astype(BF16).reshape(4, 4, 16, HALF)
        for d in OFFSETS:
            if h == 0:
                send(part.at[chain, 0, :, d], r1.at[chain, 0, d - 1], rs1_s.at[chain, 0], rs1_r.at[chain, 0], x_peer(d))
            else:
                send(part.at[chain, 1, d], r1.at[chain, 1, d - 1], rs1_s.at[chain, 1], rs1_r.at[chain, 1], y_peer(d))

    def sum_mid(chain):
        for h in range(2):
            wait(r1.at[chain, h], rs1_r.at[chain, h])
            for d in OFFSETS + (0,):
                own = part[chain, 0, d, 0] if h == 0 else part[chain, 1, 0, d]
                total = own.astype(F32)
                for j in range(3):
                    total = total + r1[chain, h, j, d].astype(F32)
                s1[chain, h, d] = total.astype(BF16)
                if d:
                    send(
                        s1.at[chain, h, d], r2.at[chain, h, d - 1], rs2_s.at[chain, h], rs2_r.at[chain, h],
                        y_peer(d) if h == 0 else x_peer(d),
                    )

    def sum_end(chain, k):
        for h in range(2):
            wait(r2.at[chain, h], rs2_r.at[chain, h])
            total = s1[chain, h, 0].astype(F32)
            for j in range(3):
                total = total + r2[chain, h, j].astype(F32)
            zs[chain, h] = total.astype(BF16)
        send(zs.at[chain], zr.at[k, chain], z_s.at[chain], z_r.at[k, chain], z_peer)

    def sum_sent(chain):
        for h in range(2):
            wait(r1.at[chain, h], rs1_s.at[chain, h])
            wait(r2.at[chain, h], rs2_s.at[chain, h])
        wait(zs.at[chain], z_s.at[chain])

    def whole_sum(chain, k):
        wait(zr.at[k, chain], z_r.at[k, chain])
        return [zs[chain, h].astype(F32) + zr[k, chain, h].astype(F32) for h in range(2)]

    def begin(chain, s):
        tick, k = s // 2, lax.rem(s, 2)
        if chain == FWD:
            gain = gain_row(1 - k)
            _, unit = norm_of(tick, k + 1)
            for h in range(2):
                gath[s, FWD, h, 0, 0] = (unit[h] * gain[:, h * HALF : (h + 1) * HALF]).astype(BF16)
        else:
            for h in range(2):
                gath[s, BWD, h, 0, 0] = rows[tick, BWD, k + 1, h]
        gather_start(chain, s)

    def hand_on(chain, k):
        @pl.when(sec > 0)
        def _():
            send(
                rows.at[0, chain, k + 2], rows.at[1, chain, k], tick_s.at[chain, k], tick_r.at[chain, k],
                {"section": sec - 1},
            )

    def take_over(chain):
        @pl.when(sec < last)
        def _():
            for k in range(2):
                wait(rows.at[1, chain, k], tick_r.at[chain, k])

    gsum[...] = jnp.zeros_like(gsum)

    for j, chain, place in places[:2]:
        unpack(0, j, 0, chain, place)
        begin(chain, 0)
    for j, chain, place in places[2:]:
        unpack(0, j, 0, chain, place)

    @pl.when(sec == last)
    def _():
        for j, chain, place in places:
            unpack(1, j, 1, chain, place)

    for copy in loads:
        copy.wait()

    def step(s, carry):
        tick, k = s // 2, lax.rem(s, 2)
        layer = 1 - k

        gather_mid(FWD, s)
        gather_mid(BWD, s)

        gather_wait(FWD, s, 0)
        hidden = dot_nn(gathered(FWD, s, 0), w_in[layer, pl.ds(0, HALF)])
        gather_wait(FWD, s, 1)
        hidden = hidden + dot_nn(gathered(FWD, s, 1), w_in[layer, pl.ds(HALF, HALF)])
        keep = masks[tick, layer].reshape(256, 256).astype(F32) * (1.0 / KEEP)
        square = hidden * hidden
        tangent = jnp.tanh(ROOT * (hidden + CUBIC * square * hidden))
        active = (0.5 * hidden * (1.0 + tangent) * keep).astype(BF16)
        for h in range(2):
            put_part(FWD, h, dot_nn(active, w_out[layer, :, pl.ds(h * HALF, HALF)]))
        slope = 0.5 * (1.0 + tangent) + 0.5 * hidden * (1.0 - tangent * tangent) * ROOT * (
            1.0 + 3.0 * CUBIC * square
        )
        slope_k[...] = slope * keep
        act_t[s] = active.astype(F32).T.astype(BF16)

        gather_wait(BWD, s, 0)
        back = dot_nt(gathered(BWD, s, 0), w_out[layer, :, pl.ds(0, HALF)])
        gather_wait(BWD, s, 1)
        back = back + dot_nt(gathered(BWD, s, 1), w_out[layer, :, pl.ds(HALF, HALF)])
        back_hidden = (back * slope_k[...]).astype(BF16)
        back_h[s] = back_hidden
        for h in range(2):
            put_part(BWD, h, dot_nt(back_hidden, w_in[layer, pl.ds(h * HALF, HALF)]))

        gather_sent(FWD, s)
        gather_sent(BWD, s)
        sum_mid(FWD)
        sum_mid(BWD)

        @pl.when(s >= 2)
        def _():
            for h in range(2):
                cols = pl.ds(h * HALF, HALF)
                g_out = dot_nn(act_t[s - 2], gathered(BWD, s - 2, h)) + dot_nn(act_t[s], gathered(BWD, s, h))
                gw_out[layer, :, cols] = g_out.astype(BF16)
                g_in = dot_tn(gathered(FWD, s - 2, h), back_h[s - 2]) + dot_tn(gathered(FWD, s, h), back_h[s])
                gw_in[layer, cols] = g_in.astype(BF16)
            pltpu.make_async_copy(gw_in.at[layer], grad_in_hbm.at[layer], out_s.at[layer, 0]).start()
            pltpu.make_async_copy(gw_out.at[layer], grad_out_hbm.at[layer], out_s.at[layer, 1]).start()

        sum_end(FWD, k)
        sum_end(BWD, k)

        branch = whole_sum(FWD, k)
        for h in range(2):
            rows[tick, FWD, k + 2, h] = (rows[tick, FWD, k, h].astype(F32) - branch[h]).astype(BF16)

        @pl.when(s == 0)
        def _():
            hand_on(FWD, 0)

        @pl.when(s == 1)
        def _():
            hand_on(FWD, 1)
            take_over(FWD)

        @pl.when(s < 3)
        def _():
            begin(FWD, s + 1)

        back_normed = whole_sum(BWD, k)
        scale, unit = norm_of(tick, k + 1)
        gain = gain_row(layer)
        back_unit = [back_normed[h] * gain[:, h * HALF : (h + 1) * HALF] for h in range(2)]
        mean = (
            jnp.sum(back_unit[0] * unit[0], axis=-1, keepdims=True)
            + jnp.sum(back_unit[1] * unit[1], axis=-1, keepdims=True)
        ) * (1.0 / (2 * HALF))
        for h in range(2):
            back_input = scale * (back_unit[h] - unit[h] * mean)
            rows[tick, BWD, k + 2, h] = (rows[tick, BWD, k, h].astype(F32) + back_input).astype(BF16)

        @pl.when(s == 0)
        def _():
            hand_on(BWD, 0)

        @pl.when(s == 1)
        def _():
            hand_on(BWD, 1)
            take_over(BWD)

        @pl.when(s < 3)
        def _():
            begin(BWD, s + 1)

        for h in range(2):
            term = jnp.sum(back_normed[h] * unit[h], axis=0, keepdims=True)
            gsum[layer, h] += jnp.broadcast_to(term, (8, HALF))
        sum_sent(FWD)
        sum_sent(BWD)
        return carry

    lax.fori_loop(0, 4, step, 0)

    row_id = lax.broadcasted_iota(jnp.int32, (8, HALF), 0)
    mine = jnp.zeros((8, HALF), F32)
    for layer in range(2):
        for h in range(2):
            mine = jnp.where(row_id == 2 * layer + h, gsum[layer, h], mine)
    grx[3] = mine
    for d in (1, 2, 3):
        send(grx.at[3], grx.at[d - 1], gx_s.at[0], gx_r.at[0], x_peer(d))

    for tick in range(2):
        for j, (chain, place) in enumerate(((FWD, 3), (FWD, 2), (BWD, 2), (BWD, 3))):
            for h in range(2):
                v = rows[tick, chain, place, h].astype(F32)
                rebuilt[tick, j, :, h * HALF : (h + 1) * HALF] = jnp.where(z == 0, v[:8], v[8:]).astype(BF16)

    wait(grx.at[pl.ds(0, 3)], gx_r.at[0])
    gry[3] = grx[3] + grx[0] + grx[1] + grx[2]
    for d in (1, 2, 3):
        send(gry.at[3], gry.at[d - 1], gx_s.at[1], gx_r.at[1], y_peer(d))
    wait(gry.at[pl.ds(0, 3)], gx_r.at[1])
    total = gry[3] + gry[0] + gry[1] + gry[2]
    for layer in range(2):
        for h in range(2):
            grad_gains[0, layer : layer + 1, h * HALF : (h + 1) * HALF] = total[2 * layer + h : 2 * layer + h + 1]

    wait(grx.at[pl.ds(0, 3)], gx_s.at[0])
    wait(gry.at[pl.ds(0, 3)], gx_s.at[1])
    for j in range(4):
        wait(hs.at[0, j], hs_s.at[j])

    @pl.when(sec == last)
    def _():
        for j in range(4):
            wait(hs.at[1, j], hs_s.at[4 + j])

    @pl.when(sec > 0)
    def _():
        for chain in range(2):
            for k in range(2):
                wait(rows.at[0, chain, k + 2], tick_s.at[chain, k])

    for layer in range(2):
        pltpu.make_async_copy(gw_in.at[layer], grad_in_hbm.at[layer], out_s.at[layer, 0]).wait()
        pltpu.make_async_copy(gw_out.at[layer], grad_out_hbm.at[layer], out_s.at[layer, 1]).wait()


def per_device(held, head, gains, w_in, w_out, masks):
    vmem = pl.BlockSpec(memory_space=pltpu.VMEM)
    anywhere = pl.BlockSpec(memory_space=pl.ANY)
    dma = pltpu.SemaphoreType.DMA
    rebuilt, grad_in, grad_out, grad_gains = pl.pallas_call(
        kernel,
        out_shape=(
            jax.ShapeDtypeStruct((2, 4, 8, 2 * HALF), BF16),
            jax.ShapeDtypeStruct((2, 2 * HALF, 256), BF16),
            jax.ShapeDtypeStruct((2, 256, 2 * HALF), BF16),
            jax.ShapeDtypeStruct((1, 2, 2 * HALF), F32),
        ),
        in_specs=[vmem, vmem, vmem, anywhere, anywhere, anywhere],
        out_specs=(vmem, anywhere, anywhere, vmem),
        scratch_shapes=[
            pltpu.VMEM((2, 2 * HALF, 256), BF16),
            pltpu.VMEM((2, 256, 2 * HALF), BF16),
            pltpu.VMEM((2, 2, 16, 2, 8, 256), jnp.int32),
            pltpu.VMEM((4, 2, 2, 4, 4, 16, HALF), BF16),
            pltpu.VMEM((2, 2, 4, 4, 16, HALF), BF16),
            pltpu.VMEM((2, 2, 3, 4, 16, HALF), BF16),
            pltpu.VMEM((2, 2, 4, 16, HALF), BF16),
            pltpu.VMEM((2, 2, 3, 16, HALF), BF16),
            pltpu.VMEM((2, 2, 16, HALF), BF16),
            pltpu.VMEM((2, 2, 2, 16, HALF), BF16),
            pltpu.VMEM((2, 2, 4, 2, 16, HALF), BF16),
            pltpu.VMEM((4, 256, 256), BF16),
            pltpu.VMEM((4, 256, 256), BF16),
            pltpu.VMEM((256, 256), F32),
            pltpu.VMEM((2, 2 * HALF, 256), BF16),
            pltpu.VMEM((2, 256, 2 * HALF), BF16),
            pltpu.VMEM((2, 4, 16, HALF), BF16),
            pltpu.VMEM((2, 4, 16, HALF), BF16),
            pltpu.VMEM((2, 2, 8, HALF), F32),
            pltpu.VMEM((4, 8, HALF), F32),
            pltpu.VMEM((4, 8, HALF), F32),
            dma((2, 2)), dma((2, 2)),
            dma((2, 2)), dma((2, 2)),
            dma((2, 2)), dma((2, 2)),
            dma((2, 2)), dma((2, 2)),
            dma((2, 2)), dma((2, 2)),
            dma((2,)), dma((2, 2)),
            dma((2, 2)), dma((2, 2)),
            dma((8,)), dma((8,)),
            dma((2,)), dma((2,)),
            dma((18,)),
            dma((2, 2)),
        ],
        compiler_params=pltpu.CompilerParams(
            collective_id=0, has_side_effects=True, vmem_limit_bytes=52 * 2**20
        ),
        name="relay",
    )(held[0], head, gains, w_in[0], w_out[0], masks.reshape(2, 2, 2, 16, 8, 256))
    return rebuilt[None], grad_in[None], grad_out[None], grad_gains


def solution(mesh):
    return jax.shard_map(
        per_device,
        mesh=mesh,
        in_specs=(
            P("section", None, "tensor", None),
            P(None, "tensor", None),
            P("section", None, None),
            P("section", None, None, "tensor"),
            P("section", None, "tensor", None),
            P("section", None, None, None, "tensor"),
        ),
        out_specs=(
            P("section", None, None, "tensor", None),
            P("section", None, None, "tensor"),
            P("section", None, "tensor", None),
            P("section", None, None),
        ),
        check_vma=False,
    )
```

time: 2030 us -> 180 us (0.09)
  waiting for transfers between devices: 1940 us -> 0 us
  Pallas kernels: 0 us -> 170 us
  other arithmetic: 32.5 us -> 0 us
  matrix products: 30.4 us -> 0 us
    psum x4 -> x0, waiting for transfers between devices: 1710 us -> none  [the longest x2 854 us: branch_backward(): lax.psum(partial_sum.astype(jnp.bfloat16), 'tensor').astype(jnp.float32)]
    all_gather x2 -> x0, waiting for transfers between devices: 228 us -> none  [run_tick(): whole = lax.all_gather(local_rows, 'tensor', axis=1, tiled=True)]
    pallas_call x0 -> x1, Pallas kernels: none -> 170 us  [per_device(): pl.pallas_call(kernel, out_shape=(jax.ShapeDtypeStruct((2, 4, 8, 2 * HALF...]
    dot_general x24 -> x0, matrix products: 30.4 us -> none  [the longest x4 5.82 us: branch_backward(): lax.dot_general(back_hidden, w_first, (((1,), (1,)), ((), ())), preferred...]
    reduce_sum x8 -> x0, other arithmetic: 21.1 us -> none  [the longest x4 11.2 us: branch_backward(): term_gain = jnp.sum(back_normed * unit, axis=0)]
  transfers between devices with their start and end apart: 7 -> 0, of which waited for: 7 -> 0; matrix products, arithmetic and copies ran while one was open for 1% -> 0% of each run, Pallas kernels for 0% -> 0%
where the time goes in v1:
time: 180 us
  Pallas kernels  170 us (94%)
  local copies, waits for them, and re-layouts  9.57 us (5%)
    pallas_call x1, Pallas kernels, per_device(): pl.pallas_call(kernel, out_shape=(jax.ShapeDtypeStruct((2, 4, 8, 2 * HALF...  170 us
    unnamed x14, local copies, waits for them, and re-layouts  9.57 us

profile of v1, /device:TPU:64, one launch (start us, length us, event | category | flops | bytes accessed | tf_op | source)
XLA Modules:
  0.0 179.9 jit_solution(15681057458590533811)
XLA Ops:
  0.6 0.0 copy-start
  0.6 1.2 copy-done
  1.9 0.0 copy-start.1
  1.9 0.9 copy-done.1
  2.8 0.0 copy-start.2
  2.8 0.9 copy-done.2
  3.7 0.0 copy-start.3
  3.7 0.7 copy-done.3
  4.4 169.7 %relay.1 = (bf16[2,4,8,2048]{3,2,1,0:T(8,128)(2,1)S(1)}, bf16[2,2048,256]{2,1,0:T(8,128)(2,1)}, bf16[2,256,2048]{2,1,0:T(8,128)(2,1)}, f32[1,2,2048]{2,1,0:T(2,128)S(1)}) custom-call(bf16[4,8,2048]{2,1,0:T(8,128)(2,1)S(1)} %bitcast.9, bf16[4,8,2048]{2,1,0:T(8,128)(2,1)S(1)} %copy-done.2, f32[1,2,2048]{2,1,0:T(2,128)S(1)} %copy-done.3, ...), custom_call_target="tpu_custom_call" | custom-call | tf_op jit(solution)/shard_map/relay/pallas_call | solution.py:401
  174.1 0.7 copy.14
  174.8 0.0 copy-start.4
  174.8 3.2 %copy.15 = bf16[1,2,2048,256]{3,2,1,0:T(8,128)(2,1)} copy(bf16[1,2,2048,256]{3,2,1,0:T(8,128)(2,1)} %bitcast.13) | data formatting | bytes 4194304
  178.0 0.0 copy-done.4
  178.0 1.3 copy.16
  179.3 0.6 copy.17
Async XLA Ops:
  0.6 1.2 copy-start
  1.9 0.9 copy-start.1
  2.8 0.9 copy-start.2
  3.7 0.7 copy-start.3
  174.8 3.2 %copy-start.4 = (bf16[2,256,2048]{2,1,0:T(8,128)(2,1)S(1)}, bf16[2,256,2048]{2,1,0:T(8,128)(2,1)}, u32[]{:S(2)}) copy-start(bf16[2,256,2048]{2,1,0:T(8,128)(2,1)} %get-tuple-element.10) | copy-start | bytes 6291460

commit v2 on v1

--- a/solution.py
+++ b/solution.py
@@ -16,7 +16,9 @@
 BF16 = jnp.bfloat16
 FWD, BWD = 0, 1
 HALF = 1024
+QUARTER = 512
 OFFSETS = (2, 1, 3)
+VMEM_BYTES = 63 * 2**20
 
 
 def dot_nn(a, b):
@@ -32,11 +34,12 @@
 
 
 def kernel(
-    held, head, gains, w_in_hbm, w_out_hbm, masks_hbm,
+    held_hbm, head_hbm, gains_hbm, w_in_hbm, w_out_hbm, masks_hbm,
     rebuilt, grad_in_hbm, grad_out_hbm, grad_gains,
-    w_in, w_out, masks, gath, part, r1, s1, r2, zs, zr, rows, act_t, back_h, slope_k,
-    gw_in, gw_out, hs, hr, gsum, grx, gry,
-    ag1_s, ag1_r, agx_s, agx_r, ag2_s, ag2_r, rs1_s, rs1_r, rs2_s, rs2_r, z_s, z_r,
+    gw_in, gw_out, held, head, gains, w_in, w_out, masks, gath, part, r1, s1, r2, zs, zr, rf, rows, act_t, back_h, slope_k,
+    hs, hr, gain_sum, grx, gry, grz,
+    ag1_s, ag1_r, agx_s, agx_r, ag2_s, agf_r, agn_r, agp_s, agp_r,
+    rs1_s, rs1_r, rsf_r, rsp_s, rsp_r, rs2_s, rs2_r, z_s, z_r,
     tick_s, tick_r, hs_s, hs_r, gx_s, gx_r, load_s, out_s,
 ):
     sec = lax.axis_index("section")
@@ -63,6 +66,11 @@
     def wait(ref, sem):
         pltpu.make_async_copy(ref, ref, sem).wait()
 
+    first_loads = [
+        pltpu.make_async_copy(held_hbm, held, load_s.at[18]),
+        pltpu.make_async_copy(head_hbm, head, load_s.at[19]),
+        pltpu.make_async_copy(gains_hbm, gains, load_s.at[20]),
+    ]
     loads = [
         pltpu.make_async_copy(w_in_hbm, w_in, load_s.at[0]),
         pltpu.make_async_copy(w_out_hbm, w_out, load_s.at[1]),
@@ -75,7 +83,7 @@
                     masks_hbm.at[:, :, :, block], masks.at[:, :, dy * 4 + dx], load_s.at[2 + dy * 4 + dx]
                 )
             )
-    for copy in loads:
+    for copy in first_loads + loads:
         copy.start()
 
     barrier = pltpu.get_barrier_semaphore()
@@ -92,6 +100,8 @@
             v = source[j].astype(F32)
             hs[slot, j] = jnp.concatenate([v[:, :HALF], v[:, HALF:]], axis=0).astype(BF16)
 
+    for copy in first_loads:
+        copy.wait()
     pack(held, 0)
 
     pl.semaphore_wait(barrier, 8)
@@ -135,49 +145,100 @@
             send(gath.at[s, chain, 0, 0, 0], gath.at[s, chain, 0, 4 - d, 0], agx_s.at[chain, 0], agx_r.at[chain, 0], y_peer(d))
             send(gath.at[s, chain, 1, 0, 0], gath.at[s, chain, 1, 0, 4 - d], agx_s.at[chain, 1], agx_r.at[chain, 1], x_peer(d))
 
+    def second_axis(h):
+        return y_peer if h == 0 else x_peer
+
+    def blocks(chain, s, h, place, q):
+        cols = pl.ds(q * QUARTER, QUARTER)
+        if h == 0:
+            return gath.at[s, chain, 0, place, pl.ds(1, 3), :, cols]
+        return gath.at[s, chain, 1, pl.ds(1, 3), place, :, cols]
+
+    def three(chain, s, h):
+        return gath.at[s, chain, h, 0, pl.ds(1, 3)]
+
     def gather_mid(chain, s):
-        wait(gath.at[s, chain, 0, 0, pl.ds(1, 3)], ag1_r.at[chain, 0])
-        for d in OFFSETS:
-            send(
-                gath.at[s, chain, 0, 0, pl.ds(1, 3)], gath.at[s, chain, 0, 4 - d, pl.ds(1, 3)],
-                ag2_s.at[chain, 0], ag2_r.at[chain, 0], y_peer(d),
-            )
-        wait(gath.at[s, chain, 1, pl.ds(1, 3), 0], ag1_r.at[chain, 1])
-        for d in OFFSETS:
-            send(
-                gath.at[s, chain, 1, pl.ds(1, 3), 0], gath.at[s, chain, 1, pl.ds(1, 3), 4 - d],
-                ag2_s.at[chain, 1], ag2_r.at[chain, 1], x_peer(d),
-            )
+        for h in range(2):
+            wait(three(chain, s, h), ag1_r.at[chain, h])
+        for q in range(2):
+            for h in range(2):
+                peer = second_axis(h)
+                for right in range(2):
+                    cols = q if right else 1 - q
+                    r_sem = agf_r.at[chain, h, right] if q == 0 else agn_r.at[chain, h]
+                    send(
+                        blocks(chain, s, h, 0, cols), blocks(chain, s, h, 3 if right else 1, cols),
+                        ag2_s.at[chain, h], r_sem, peer(1 if right else 3),
+                    )
+
+    def gather_pass(chain, s):
+        for right in (1, 0):
+            for h in range(2):
+                cols = 0 if right else 1
+                came = blocks(chain, s, h, 3 if right else 1, cols)
+                wait(came, agf_r.at[chain, h, right])
+                send(
+                    came, blocks(chain, s, h, 2, cols), agp_s.at[chain, h], agp_r.at[chain, h],
+                    second_axis(h)(1 if right else 3),
+                )
 
     def gather_wait(chain, s, h):
-        wait(gath.at[s, chain, h, 0, pl.ds(1, 3)], agx_r.at[chain, h])
-        wait(gath.at[s, chain, h, pl.ds(1, 3), pl.ds(1, 3)], ag2_r.at[chain, h])
+        wait(three(chain, s, h), agx_r.at[chain, h])
+        wait(three(chain, s, h), agn_r.at[chain, h])
+        wait(three(chain, s, h), agp_r.at[chain, h])
 
     def gather_sent(chain, s):
         for h in range(2):
-            wait(gath.at[s, chain, h, 0, pl.ds(1, 3)], ag1_s.at[chain, h])
-            wait(gath.at[s, chain, h, 0, pl.ds(1, 3)], agx_s.at[chain, h])
-            wait(gath.at[s, chain, h, pl.ds(1, 3), pl.ds(1, 3)], ag2_s.at[chain, h])
+            wait(three(chain, s, h), ag1_s.at[chain, h])
+            wait(three(chain, s, h), agx_s.at[chain, h])
+            wait(gath.at[s, chain, h, pl.ds(0, 2), pl.ds(1, 3)], ag2_s.at[chain, h])
+            wait(three(chain, s, h), agp_s.at[chain, h])
 
     def gathered(chain, s, h):
         return gath[s, chain, h].reshape(256, HALF)
 
+    def first_axis(h):
+        return x_peer if h == 0 else y_peer
+
+    def strip(chain, h, d, q):
+        cols = pl.ds(q * QUARTER, QUARTER)
+        if h == 0:
+            return part.at[chain, 0, :, d, :, cols]
+        return part.at[chain, 1, d, :, :, cols]
+
     def put_part(chain, h, value):
         part[chain, h] = value.astype(BF16).reshape(4, 4, 16, HALF)
-        for d in OFFSETS:
-            if h == 0:
-                send(part.at[chain, 0, :, d], r1.at[chain, 0, d - 1], rs1_s.at[chain, 0], rs1_r.at[chain, 0], x_peer(d))
-            else:
-                send(part.at[chain, 1, d], r1.at[chain, 1, d - 1], rs1_s.at[chain, 1], rs1_r.at[chain, 1], y_peer(d))
+        peer = first_axis(h)
+        for right in (1, 0):
+            send(
+                strip(chain, h, 2, 1 - right), rf.at[chain, h, right],
+                rs1_s.at[chain, h], rsf_r.at[chain, h, right], peer(1 if right else 3),
+            )
+        for right in (1, 0):
+            send(
+                strip(chain, h, 1 if right else 3, right), r1.at[chain, h, right, :, :, pl.ds(right * QUARTER, QUARTER)],
+                rs1_s.at[chain, h], rs1_r.at[chain, h], peer(1 if right else 3),
+            )
+
+    def sum_pass(chain):
+        for right in (1, 0):
+            for h in range(2):
+                d, q = (1, 0) if right else (3, 1)
+                wait(rf.at[chain, h, right], rsf_r.at[chain, h, right])
+                own = strip(chain, h, d, q)
+                own[...] = (own[...].astype(F32) + rf[chain, h, right].astype(F32)).astype(BF16)
+                send(
+                    own, r1.at[chain, h, right, :, :, pl.ds(q * QUARTER, QUARTER)],
+                    rsp_s.at[chain, h], rsp_r.at[chain, h], first_axis(h)(1 if right else 3),
+                )
 
     def sum_mid(chain):
         for h in range(2):
-            wait(r1.at[chain, h], rs1_r.at[chain, h])
+            wait(r1.at[chain, h, 0], rs1_r.at[chain, h])
+            wait(r1.at[chain, h, 0], rsp_r.at[chain, h])
             for d in OFFSETS + (0,):
                 own = part[chain, 0, d, 0] if h == 0 else part[chain, 1, 0, d]
-                total = own.astype(F32)
-                for j in range(3):
-                    total = total + r1[chain, h, j, d].astype(F32)
+                total = own.astype(F32) + (r1[chain, h, 0, d].astype(F32) + r1[chain, h, 1, d].astype(F32))
                 s1[chain, h, d] = total.astype(BF16)
                 if d:
                     send(
@@ -197,6 +258,7 @@
     def sum_sent(chain):
         for h in range(2):
             wait(r1.at[chain, h], rs1_s.at[chain, h])
+            wait(r1.at[chain, h, 0], rsp_s.at[chain, h])
             wait(r2.at[chain, h], rs2_s.at[chain, h])
         wait(zs.at[chain], z_s.at[chain])
 
@@ -230,8 +292,6 @@
             for k in range(2):
                 wait(rows.at[1, chain, k], tick_r.at[chain, k])
 
-    gsum[...] = jnp.zeros_like(gsum)
-
     for j, chain, place in places[:2]:
         unpack(0, j, 0, chain, place)
         begin(chain, 0)
@@ -246,13 +306,9 @@
     for copy in loads:
         copy.wait()
 
-    def step(s, carry):
+    def forward(s):
         tick, k = s // 2, lax.rem(s, 2)
         layer = 1 - k
-
-        gather_mid(FWD, s)
-        gather_mid(BWD, s)
-
         gather_wait(FWD, s, 0)
         hidden = dot_nn(gathered(FWD, s, 0), w_in[layer, pl.ds(0, HALF)])
         gather_wait(FWD, s, 1)
@@ -269,6 +325,8 @@
         slope_k[...] = slope * keep
         act_t[s] = active.astype(F32).T.astype(BF16)
 
+    def backward(s):
+        layer = 1 - lax.rem(s, 2)
         gather_wait(BWD, s, 0)
         back = dot_nt(gathered(BWD, s, 0), w_out[layer, :, pl.ds(0, HALF)])
         gather_wait(BWD, s, 1)
@@ -278,45 +336,17 @@
         for h in range(2):
             put_part(BWD, h, dot_nt(back_hidden, w_in[layer, pl.ds(h * HALF, HALF)]))
 
-        gather_sent(FWD, s)
-        gather_sent(BWD, s)
-        sum_mid(FWD)
-        sum_mid(BWD)
-
-        @pl.when(s >= 2)
-        def _():
-            for h in range(2):
-                cols = pl.ds(h * HALF, HALF)
-                g_out = dot_nn(act_t[s - 2], gathered(BWD, s - 2, h)) + dot_nn(act_t[s], gathered(BWD, s, h))
-                gw_out[layer, :, cols] = g_out.astype(BF16)
-                g_in = dot_tn(gathered(FWD, s - 2, h), back_h[s - 2]) + dot_tn(gathered(FWD, s, h), back_h[s])
-                gw_in[layer, cols] = g_in.astype(BF16)
-            pltpu.make_async_copy(gw_in.at[layer], grad_in_hbm.at[layer], out_s.at[layer, 0]).start()
-            pltpu.make_async_copy(gw_out.at[layer], grad_out_hbm.at[layer], out_s.at[layer, 1]).start()
-
-        sum_end(FWD, k)
-        sum_end(BWD, k)
-
+    def forward_rows(s):
+        tick, k = s // 2, lax.rem(s, 2)
         branch = whole_sum(FWD, k)
         for h in range(2):
             rows[tick, FWD, k + 2, h] = (rows[tick, FWD, k, h].astype(F32) - branch[h]).astype(BF16)
 
-        @pl.when(s == 0)
-        def _():
-            hand_on(FWD, 0)
-
-        @pl.when(s == 1)
-        def _():
-            hand_on(FWD, 1)
-            take_over(FWD)
-
-        @pl.when(s < 3)
-        def _():
-            begin(FWD, s + 1)
-
+    def backward_rows(s):
+        tick, k = s // 2, lax.rem(s, 2)
+        scale, unit = norm_of(tick, k + 1)
+        gain = gain_row(1 - k)
         back_normed = whole_sum(BWD, k)
-        scale, unit = norm_of(tick, k + 1)
-        gain = gain_row(layer)
         back_unit = [back_normed[h] * gain[:, h * HALF : (h + 1) * HALF] for h in range(2)]
         mean = (
             jnp.sum(back_unit[0] * unit[0], axis=-1, keepdims=True)
@@ -326,55 +356,114 @@
             back_input = scale * (back_unit[h] - unit[h] * mean)
             rows[tick, BWD, k + 2, h] = (rows[tick, BWD, k, h].astype(F32) + back_input).astype(BF16)
 
+    def next_rows(chain, s):
         @pl.when(s == 0)
         def _():
-            hand_on(BWD, 0)
+            hand_on(chain, 0)
 
         @pl.when(s == 1)
         def _():
-            hand_on(BWD, 1)
-            take_over(BWD)
+            hand_on(chain, 1)
+            take_over(chain)
 
         @pl.when(s < 3)
         def _():
-            begin(BWD, s + 1)
-
-        for h in range(2):
-            term = jnp.sum(back_normed[h] * unit[h], axis=0, keepdims=True)
-            gsum[layer, h] += jnp.broadcast_to(term, (8, HALF))
+            begin(chain, s + 1)
+
+    def grad_out(layer):
+        for h in range(2):
+            first, second = 1 - layer, 3 - layer
+            g_out = dot_nn(act_t[first], gathered(BWD, first, h)) + dot_nn(act_t[second], gathered(BWD, second, h))
+            gw_out[layer, :, pl.ds(h * HALF, HALF)] = g_out.astype(BF16)
+
+    def grad_in(layer):
+        for h in range(2):
+            first, second = 1 - layer, 3 - layer
+            span = pl.ds(h * HALF, HALF)
+            g_in = dot_tn(gathered(FWD, first, h), back_h[first]) + dot_tn(gathered(FWD, second, h), back_h[second])
+            gw_in[layer, span] = g_in.astype(BF16)
+            product = (g_in * w_in[layer, span].astype(F32)).astype(BF16)
+            sums = dot_nt(jnp.ones((8, 256), BF16), product)
+            gain_sum[2 * layer + h] = sums / gains[0, layer : layer + 1, h * HALF : (h + 1) * HALF]
+
+    def out_copy(layer, which):
+        if which == 0:
+            return pltpu.make_async_copy(gw_in.at[layer], grad_in_hbm.at[layer], out_s.at[layer, 0])
+        return pltpu.make_async_copy(gw_out.at[layer], grad_out_hbm.at[layer], out_s.at[layer, 1])
+
+    def put_rows(tick, j):
+        chain, place = ((FWD, 3), (FWD, 2), (BWD, 2), (BWD, 3))[j]
+        for h in range(2):
+            v = rows[tick, chain, place, h].astype(F32)
+            rebuilt[tick, j, :, h * HALF : (h + 1) * HALF] = jnp.where(z == 0, v[:8], v[8:]).astype(BF16)
+
+    def while_first_sum():
+        for layer in (1, 0):
+            grad_in(layer)
+            out_copy(layer, 0).start()
+        mine = [gain_sum[j, 0:1] for j in range(4)]
+        grx[x] = jnp.concatenate(mine + mine, axis=0)
+        for d in (1, 2, 3):
+            send(grx.at[x], grx.at[x], gx_s.at[0], gx_r.at[0], x_peer(d))
+
+    def while_second_sum():
+        wait(grx.at[pl.ds(0, 3)], gx_r.at[0])
+        gry[y] = (grx[0] + grx[1]) + (grx[2] + grx[3])
+        for d in (1, 2, 3):
+            send(gry.at[y], gry.at[y], gx_s.at[1], gx_r.at[1], y_peer(d))
+        for layer in (1, 0):
+            grad_out(layer)
+            out_copy(layer, 1).start()
+
+    def while_third_sum():
+        wait(gry.at[pl.ds(0, 3)], gx_r.at[1])
+        grz[0] = (gry[0] + gry[1]) + (gry[2] + gry[3])
+        send(grz.at[0], grz.at[1], gx_s.at[2], gx_r.at[2], z_peer)
+        for j in range(4):
+            put_rows(0, j)
+        put_rows(1, 1)
+        put_rows(1, 2)
+
+    def step(s, carry):
+        k = lax.rem(s, 2)
+        gather_mid(FWD, s)
+        gather_mid(BWD, s)
+        gather_pass(FWD, s)
+        gather_pass(BWD, s)
+        forward(s)
+        backward(s)
+        sum_pass(FWD)
+        sum_pass(BWD)
+        pl.when(s == 3)(while_first_sum)
+        gather_sent(FWD, s)
+        gather_sent(BWD, s)
+        sum_mid(FWD)
+        sum_mid(BWD)
+        pl.when(s == 3)(while_second_sum)
+        sum_end(FWD, k)
+        sum_end(BWD, k)
+        pl.when(s == 3)(while_third_sum)
+        forward_rows(s)
+        next_rows(FWD, s)
+        backward_rows(s)
+        next_rows(BWD, s)
         sum_sent(FWD)
         sum_sent(BWD)
         return carry
 
     lax.fori_loop(0, 4, step, 0)
 
-    row_id = lax.broadcasted_iota(jnp.int32, (8, HALF), 0)
-    mine = jnp.zeros((8, HALF), F32)
-    for layer in range(2):
-        for h in range(2):
-            mine = jnp.where(row_id == 2 * layer + h, gsum[layer, h], mine)
-    grx[3] = mine
-    for d in (1, 2, 3):
-        send(grx.at[3], grx.at[d - 1], gx_s.at[0], gx_r.at[0], x_peer(d))
-
-    for tick in range(2):
-        for j, (chain, place) in enumerate(((FWD, 3), (FWD, 2), (BWD, 2), (BWD, 3))):
-            for h in range(2):
-                v = rows[tick, chain, place, h].astype(F32)
-                rebuilt[tick, j, :, h * HALF : (h + 1) * HALF] = jnp.where(z == 0, v[:8], v[8:]).astype(BF16)
-
-    wait(grx.at[pl.ds(0, 3)], gx_r.at[0])
-    gry[3] = grx[3] + grx[0] + grx[1] + grx[2]
-    for d in (1, 2, 3):
-        send(gry.at[3], gry.at[d - 1], gx_s.at[1], gx_r.at[1], y_peer(d))
-    wait(gry.at[pl.ds(0, 3)], gx_r.at[1])
-    total = gry[3] + gry[0] + gry[1] + gry[2]
+    put_rows(1, 0)
+    put_rows(1, 3)
+    wait(grz.at[1], gx_r.at[2])
+    total = grz[0] + grz[1]
     for layer in range(2):
         for h in range(2):
             grad_gains[0, layer : layer + 1, h * HALF : (h + 1) * HALF] = total[2 * layer + h : 2 * layer + h + 1]
 
     wait(grx.at[pl.ds(0, 3)], gx_s.at[0])
     wait(gry.at[pl.ds(0, 3)], gx_s.at[1])
+    wait(grz.at[0], gx_s.at[2])
     for j in range(4):
         wait(hs.at[0, j], hs_s.at[j])
 
@@ -390,63 +479,102 @@
                 wait(rows.at[0, chain, k + 2], tick_s.at[chain, k])
 
     for layer in range(2):
-        pltpu.make_async_copy(gw_in.at[layer], grad_in_hbm.at[layer], out_s.at[layer, 0]).wait()
-        pltpu.make_async_copy(gw_out.at[layer], grad_out_hbm.at[layer], out_s.at[layer, 1]).wait()
+        for which in range(2):
+            out_copy(layer, which).wait()
+
+
+def write_out(*refs):
+    sources, results, held, sems = refs[:4], refs[4:8], refs[8:12], refs[12]
+
+    def pieces(first, second):
+        found = [(0, ...), (3, ...)]
+        for layer in range(2):
+            for j in range(4):
+                found.append((1, (layer, pl.ds(512 * j, 512))))
+                found.append((2, (layer, pl.ds(64 * j, 64))))
+        return [
+            pltpu.make_async_copy(first[i].at[at], second[i].at[at], sems.at[n, 0 if second is held else 1])
+            for n, (i, at) in enumerate(found)
+        ]
+
+    loads, stores = pieces(sources, held), pieces(held, results)
+    for load in loads:
+        load.start()
+    for load, store in zip(loads, stores):
+        load.wait()
+        store.start()
+    for store in stores:
+        store.wait()
 
 
 def per_device(held, head, gains, w_in, w_out, masks):
     vmem = pl.BlockSpec(memory_space=pltpu.VMEM)
     anywhere = pl.BlockSpec(memory_space=pl.ANY)
     dma = pltpu.SemaphoreType.DMA
-    rebuilt, grad_in, grad_out, grad_gains = pl.pallas_call(
+    shapes = (
+        jax.ShapeDtypeStruct((2, 4, 8, 2 * HALF), BF16),
+        jax.ShapeDtypeStruct((2, 2 * HALF, 256), BF16),
+        jax.ShapeDtypeStruct((2, 256, 2 * HALF), BF16),
+        jax.ShapeDtypeStruct((1, 2, 2 * HALF), F32),
+    )
+    results = pl.pallas_call(
         kernel,
-        out_shape=(
-            jax.ShapeDtypeStruct((2, 4, 8, 2 * HALF), BF16),
-            jax.ShapeDtypeStruct((2, 2 * HALF, 256), BF16),
-            jax.ShapeDtypeStruct((2, 256, 2 * HALF), BF16),
-            jax.ShapeDtypeStruct((1, 2, 2 * HALF), F32),
-        ),
-        in_specs=[vmem, vmem, vmem, anywhere, anywhere, anywhere],
+        out_shape=shapes,
+        in_specs=[anywhere] * 6,
         out_specs=(vmem, anywhere, anywhere, vmem),
         scratch_shapes=[
+            pltpu.VMEM((2, 2 * HALF, 256), BF16),
+            pltpu.VMEM((2, 256, 2 * HALF), BF16),
+            pltpu.VMEM((4, 8, 2 * HALF), BF16),
+            pltpu.VMEM((4, 8, 2 * HALF), BF16),
+            pltpu.VMEM((1, 2, 2 * HALF), F32),
             pltpu.VMEM((2, 2 * HALF, 256), BF16),
             pltpu.VMEM((2, 256, 2 * HALF), BF16),
             pltpu.VMEM((2, 2, 16, 2, 8, 256), jnp.int32),
             pltpu.VMEM((4, 2, 2, 4, 4, 16, HALF), BF16),
             pltpu.VMEM((2, 2, 4, 4, 16, HALF), BF16),
-            pltpu.VMEM((2, 2, 3, 4, 16, HALF), BF16),
+            pltpu.VMEM((2, 2, 2, 4, 16, HALF), BF16),
             pltpu.VMEM((2, 2, 4, 16, HALF), BF16),
             pltpu.VMEM((2, 2, 3, 16, HALF), BF16),
             pltpu.VMEM((2, 2, 16, HALF), BF16),
             pltpu.VMEM((2, 2, 2, 16, HALF), BF16),
+            pltpu.VMEM((2, 2, 2, 4, 16, QUARTER), BF16),
             pltpu.VMEM((2, 2, 4, 2, 16, HALF), BF16),
             pltpu.VMEM((4, 256, 256), BF16),
             pltpu.VMEM((4, 256, 256), BF16),
             pltpu.VMEM((256, 256), F32),
-            pltpu.VMEM((2, 2 * HALF, 256), BF16),
-            pltpu.VMEM((2, 256, 2 * HALF), BF16),
             pltpu.VMEM((2, 4, 16, HALF), BF16),
             pltpu.VMEM((2, 4, 16, HALF), BF16),
-            pltpu.VMEM((2, 2, 8, HALF), F32),
             pltpu.VMEM((4, 8, HALF), F32),
             pltpu.VMEM((4, 8, HALF), F32),
+            pltpu.VMEM((4, 8, HALF), F32),
+            pltpu.VMEM((2, 8, HALF), F32),
             dma((2, 2)), dma((2, 2)),
             dma((2, 2)), dma((2, 2)),
-            dma((2, 2)), dma((2, 2)),
-            dma((2, 2)), dma((2, 2)),
+            dma((2, 2)), dma((2, 2, 2)), dma((2, 2)), dma((2, 2)), dma((2, 2)),
+            dma((2, 2)), dma((2, 2)), dma((2, 2, 2)), dma((2, 2)), dma((2, 2)),
             dma((2, 2)), dma((2, 2)),
             dma((2,)), dma((2, 2)),
             dma((2, 2)), dma((2, 2)),
             dma((8,)), dma((8,)),
-            dma((2,)), dma((2,)),
-            dma((18,)),
+            dma((3,)), dma((3,)),
+            dma((21,)),
             dma((2, 2)),
         ],
         compiler_params=pltpu.CompilerParams(
-            collective_id=0, has_side_effects=True, vmem_limit_bytes=52 * 2**20
+            collective_id=0, has_side_effects=True, vmem_limit_bytes=VMEM_BYTES
         ),
         name="relay",
     )(held[0], head, gains, w_in[0], w_out[0], masks.reshape(2, 2, 2, 16, 8, 256))
+    rebuilt, grad_in, grad_out, grad_gains = pl.pallas_call(
+        write_out,
+        out_shape=shapes,
+        in_specs=[anywhere] * 4,
+        out_specs=(anywhere,) * 4,
+        scratch_shapes=[pltpu.VMEM(shape.shape, shape.dtype) for shape in shapes] + [dma((18, 2))],
+        compiler_params=pltpu.CompilerParams(vmem_limit_bytes=VMEM_BYTES),
+        name="write_out",
+    )(*results)
     return rebuilt[None], grad_in[None], grad_out[None], grad_gains
 
 

time: 180 us -> 161 us (0.89)
  Pallas kernels: 170 us -> 160 us
  local copies, waits for them, and re-layouts: 9.57 us -> 0 us
    unnamed x14 -> x0, local copies, waits for them, and re-layouts: 9.57 us -> none
    pallas_call x1 -> x2, Pallas kernels: 170 us -> 160 us  [the longest x1 156 us: per_device(): pl.pallas_call(kernel, out_shape=shapes, in_specs=[anywhere] * 6, out_spe...]
where the time goes in v2:
time: 161 us
  Pallas kernels  160 us (99%)
    pallas_call x1, Pallas kernels, per_device(): pl.pallas_call(kernel, out_shape=shapes, in_specs=[anywhere] * 6, out_spe...  156 us
    pallas_call x1, Pallas kernels, per_device(): pl.pallas_call(write_out, out_shape=shapes, in_specs=[anywhere] * 4, out_...  4.2 us

profile of v2, /device:TPU:64, one launch (start us, length us, event | category | flops | bytes accessed | tf_op | source)
XLA Modules:
  0.0 160.9 jit_solution(14538366012147722424)
XLA Ops:
  0.6 156.0 %relay.1 = (bf16[2,4,8,2048]{3,2,1,0:T(8,128)(2,1)}, bf16[2,2048,256]{2,1,0:T(8,128)(2,1)}, bf16[2,256,2048]{2,1,0:T(8,128)(2,1)}, f32[1,2,2048]{2,1,0:T(2,128)}) custom-call(bf16[4,8,2048]{2,1,0:T(8,128)(2,1)} %bitcast.10, bf16[4,8,2048]{2,1,0:T(8,128)(2,1)} %head_hbm.1, f32[1,2,2048]{2,1,0:T(2,128)} %gains_hbm.1, bf16[2,2048,256]{2,1,0:T(8,128)(2,1)} %bitcast.7, ...), custom_call_target="tpu_custom_call" | custom-call | tf_op jit(solution)/shard_map/relay/pallas_call | solution.py:520
  156.7 4.2 %write_out.1 = (bf16[2,4,8,2048]{3,2,1,0:T(8,128)(2,1)}, bf16[2,2048,256]{2,1,0:T(8,128)(2,1)}, bf16[2,256,2048]{2,1,0:T(8,128)(2,1)}, f32[1,2,2048]{2,1,0:T(2,128)}) custom-call(bf16[2,4,8,2048]{3,2,1,0:T(8,128)(2,1)} %get-tuple-element.12.refs_0_, bf16[2,2048,256]{2,1,0:T(8,128)(2,1)} %get-tuple-element.13.refs_1_, ...), custom_call_target="tpu_custom_call" | custom-call | tf_op jit(solution)/shard_map/write_out/pallas_call | solution.py:569

commit v3 on v2

--- a/solution.py
+++ b/solution.py
@@ -253,7 +253,7 @@
             for j in range(3):
                 total = total + r2[chain, h, j].astype(F32)
             zs[chain, h] = total.astype(BF16)
-        send(zs.at[chain], zr.at[k, chain], z_s.at[chain], z_r.at[k, chain], z_peer)
+            send(zs.at[chain, h], zr.at[k, chain, h], z_s.at[chain], z_r.at[k, chain], z_peer)
 
     def sum_sent(chain):
         for h in range(2):
@@ -356,19 +356,22 @@
             back_input = scale * (back_unit[h] - unit[h] * mean)
             rows[tick, BWD, k + 2, h] = (rows[tick, BWD, k, h].astype(F32) + back_input).astype(BF16)
 
-    def next_rows(chain, s):
-        @pl.when(s == 0)
-        def _():
-            hand_on(chain, 0)
+    def rows_and_next(s):
+        forward_rows(s)
+        for k in range(2):
+            pl.when(s == k)(lambda k=k: hand_on(FWD, k))
+        pl.when(lax.rem(s, 2) == 0)(lambda: begin(FWD, s + 1))
+        pl.when(s == 3)(lambda: put_rows(1, 0))
+        backward_rows(s)
+        for k in range(2):
+            pl.when(s == k)(lambda k=k: hand_on(BWD, k))
+        pl.when(lax.rem(s, 2) == 0)(lambda: begin(BWD, s + 1))
 
         @pl.when(s == 1)
         def _():
-            hand_on(chain, 1)
-            take_over(chain)
-
-        @pl.when(s < 3)
-        def _():
-            begin(chain, s + 1)
+            for chain in (FWD, BWD):
+                take_over(chain)
+                begin(chain, 2)
 
     def grad_out(layer):
         for h in range(2):
@@ -443,17 +446,13 @@
         sum_end(FWD, k)
         sum_end(BWD, k)
         pl.when(s == 3)(while_third_sum)
-        forward_rows(s)
-        next_rows(FWD, s)
-        backward_rows(s)
-        next_rows(BWD, s)
+        rows_and_next(s)
         sum_sent(FWD)
         sum_sent(BWD)
         return carry
 
     lax.fori_loop(0, 4, step, 0)
 
-    put_rows(1, 0)
     put_rows(1, 3)
     wait(grz.at[1], gx_r.at[2])
     total = grz[0] + grz[1]

time: 161 us -> 161 us (level)
  no operation moved by 1% of the time
where the time goes in v3:
time: 161 us
  Pallas kernels  160 us (99%)
    pallas_call x1, Pallas kernels, per_device(): pl.pallas_call(kernel, out_shape=shapes, in_specs=[anywhere] * 6, out_spe...  156 us
    pallas_call x1, Pallas kernels, per_device(): pl.pallas_call(write_out, out_shape=shapes, in_specs=[anywhere] * 4, out_...  4.2 us

profile of v3, /device:TPU:64, one launch (start us, length us, event | category | flops | bytes accessed | tf_op | source)
XLA Modules:
  0.0 160.6 jit_solution(492311574483621657)
XLA Ops:
  0.6 155.7 %relay.1 = (bf16[2,4,8,2048]{3,2,1,0:T(8,128)(2,1)}, bf16[2,2048,256]{2,1,0:T(8,128)(2,1)}, bf16[2,256,2048]{2,1,0:T(8,128)(2,1)}, f32[1,2,2048]{2,1,0:T(2,128)}) custom-call(bf16[4,8,2048]{2,1,0:T(8,128)(2,1)} %bitcast.10, bf16[4,8,2048]{2,1,0:T(8,128)(2,1)} %head_hbm.1, f32[1,2,2048]{2,1,0:T(2,128)} %gains_hbm.1, bf16[2,2048,256]{2,1,0:T(8,128)(2,1)} %bitcast.7, ...), custom_call_target="tpu_custom_call" | custom-call | tf_op jit(solution)/shard_map/relay/pallas_call | solution.py:519
  156.4 4.2 %write_out.1 = (bf16[2,4,8,2048]{3,2,1,0:T(8,128)(2,1)}, bf16[2,2048,256]{2,1,0:T(8,128)(2,1)}, bf16[2,256,2048]{2,1,0:T(8,128)(2,1)}, f32[1,2,2048]{2,1,0:T(2,128)}) custom-call(bf16[2,4,8,2048]{3,2,1,0:T(8,128)(2,1)} %get-tuple-element.12.refs_0_, bf16[2,2048,256]{2,1,0:T(8,128)(2,1)} %get-tuple-element.13.refs_1_, ...), custom_call_target="tpu_custom_call" | custom-call | tf_op jit(solution)/shard_map/write_out/pallas_call | solution.py:568
